TPU v7x, 32 devices: a whole 2x2x4 slice. The times are simulated.
32 devices in a mesh: row: 4 (over y, core), col: 8 (over z, x).
Axes of the slice: x: 2, y: 2, z: 4, core: 2. Of those that a mesh axis runs over, the one named last changes fastest.
Arguments:
- forward_head: bfloat16 [4, 2048, 1000], P(None, 'col'), may hold values from -6 to 6
- forward_tail: bfloat16 [57344, 1000], P(('col', 'row')), may hold values from -6 to 6
- forward_inverse: bfloat16 [4, 2048, 2048], P(None, 'col', 'row'), may hold values from -1.5 to 1.5, as said below
- forward_coupling: bfloat16 [6, 2048, 2048], P(None, 'row', 'col'), may hold values from -0.078125 to 0.078125
- forward_slab: bfloat16 [4, 2048, 57344], P(None, 'row', 'col'), may hold values from -0.0625 to 0.0625
- backward_head: bfloat16 [4, 2048, 1000], P(None, 'row'), may hold values from -6 to 6
- backward_tail: bfloat16 [57344, 1000], P(('row', 'col')), may hold values from -6 to 6
- backward_inverse: bfloat16 [4, 2048, 2048], P(None, 'col', 'row'), may hold values from -1.5 to 1.5, as said below
- backward_coupling: bfloat16 [6, 2048, 2048], P(None, 'row', 'col'), may hold values from -0.078125 to 0.078125
- backward_slab: bfloat16 [57344, 4, 2048], P('row', None, 'col'), may hold values from -0.0625 to 0.0625
Outputs:
- lower_head: bfloat16 [4, 2048, 1000], P(None, 'row')
- lower_tail: bfloat16 [57344, 1000], P(('col', 'row'))
- upper_head: bfloat16 [4, 2048, 1000], P(None, 'col')
- upper_tail: bfloat16 [57344, 1000], P(('row', 'col'))
Inputs may be any that keep to these rules, and one draw needn't show every extreme that they name: Each block of forward_inverse is upper triangular with diagonal entries of magnitude 0.5 to 1.5. Each block of backward_inverse is upper triangular with diagonal entries of magnitude 0.5 to 1.5.
All inputs are finite; a program needn't handle non-finite values.
Results may differ from a plain program's by a relative error of at most 0.03.
Values may be sent and summed in bfloat16 or wider, within the bound.
A program may use at most 192 MiB of HBM per device.

v0:
```python
import jax
import jax.numpy as jnp
from jax import lax
from jax.sharding import PartitionSpec as P


def reduce_row(value):
    return lax.psum(value.astype(jnp.bfloat16), "row").astype(jnp.float32)


def reduce_col(value):
    return lax.psum(value.astype(jnp.bfloat16), "col").astype(jnp.float32)


def leading_dot(left, right):
    return lax.dot_general(
        left, right, (((0,), (0,)), ((), ())), preferred_element_type=jnp.float32
    )


def local(
    forward_head,
    forward_tail,
    forward_inverse,
    forward_coupling,
    forward_slab,
    backward_head,
    backward_tail,
    backward_inverse,
    backward_coupling,
    backward_slab,
):
    classes = forward_head.shape[2]
    panels = forward_head.shape[0]
    lower_list = []
    for panel_index in range(panels):
        if panel_index == 0:
            adjusted = forward_head[0]
        else:
            summed = leading_dot(
                forward_coupling[panel_index * (panel_index - 1) // 2], lower_list[0]
            )
            for earlier in range(1, panel_index):
                summed = summed + leading_dot(
                    forward_coupling[panel_index * (panel_index - 1) // 2 + earlier],
                    lower_list[earlier],
                )
            coupling = reduce_row(summed)
            adjusted = (forward_head[panel_index].astype(jnp.float32) - coupling).astype(
                jnp.bfloat16
            )
        lower_list.append(
            reduce_col(leading_dot(forward_inverse[panel_index], adjusted)).astype(jnp.bfloat16)
        )
    lower_head = jnp.stack(lower_list)
    panel_rows = lower_head.shape[1]
    flat_lower = lower_head.reshape(panels * panel_rows, classes)
    flat_slab = forward_slab.reshape(panels * panel_rows, forward_slab.shape[2])
    lower_update = lax.psum_scatter(
        leading_dot(flat_slab, flat_lower).astype(jnp.bfloat16),
        "row",
        scatter_dimension=0,
        tiled=True,
    ).astype(jnp.float32)
    lower_tail = (forward_tail.astype(jnp.float32) - lower_update).astype(jnp.bfloat16)
    upper_list = [None] * panels
    for panel_index in reversed(range(panels)):
        if panel_index == panels - 1:
            shifted = backward_head[panel_index]
        else:
            summed = None
            for later_panel in range(panel_index + 1, panels):
                block = backward_coupling[later_panel * (later_panel - 1) // 2 + panel_index]
                product = jnp.dot(
                    block, upper_list[later_panel], preferred_element_type=jnp.float32
                )
                summed = product if summed is None else summed + product
            pulled = reduce_col(summed)
            shifted = (backward_head[panel_index].astype(jnp.float32) - pulled).astype(jnp.bfloat16)
        upper_list[panel_index] = reduce_row(
            jnp.dot(backward_inverse[panel_index], shifted, preferred_element_type=jnp.float32)
        ).astype(jnp.bfloat16)
    upper_head = jnp.stack(upper_list)
    panel_cols = upper_head.shape[1]
    flat_back = backward_slab.reshape(backward_slab.shape[0], panels * panel_cols)
    flat_upper = upper_head.reshape(panels * panel_cols, classes)
    upper_update = lax.psum_scatter(
        jnp.dot(flat_back, flat_upper, preferred_element_type=jnp.float32).astype(jnp.bfloat16),
        "col",
        scatter_dimension=0,
        tiled=True,
    ).astype(jnp.float32)
    upper_tail = (backward_tail.astype(jnp.float32) - upper_update).astype(jnp.bfloat16)
    return (lower_head, lower_tail, upper_head, upper_tail)


def solution(mesh):
    in_specs = (
        P(None, "col", None),
        P(("col", "row"), None),
        P(None, "col", "row"),
        P(None, "row", "col"),
        P(None, "row", "col"),
        P(None, "row", None),
        P(("row", "col"), None),
        P(None, "col", "row"),
        P(None, "row", "col"),
        P("row", None, "col"),
    )
    out_specs = (
        P(None, "row", None),
        P(("col", "row"), None),
        P(None, "col", None),
        P(("row", "col"), None),
    )
    return jax.shard_map(local, mesh=mesh, in_specs=in_specs, out_specs=out_specs, check_vma=False)
```

profile of v0, /device:TPU:0, one launch (start us, length us, event | category | flops | bytes accessed | tf_op | source)
XLA Modules:
  0.0 1229.3 jit_solution(1852988721741176343)
XLA Ops:
  7.2 2.5 convolution_convert_fusion.4
  9.8 2.6 convolution_convert_fusion.8
  12.4 80.2 %all-reduce.15.cloned.1.call-done = bf16[512,1000]{0,1:T(8,128)(2,1)} async-done(((bf16[512,1000]{0,1:T(8,128)(2,1)}), bf16[512,1000]{0,1:T(8,128)(2,1)}) %all-reduce.15.cloned.1.call-update) | async-done | bytes 1024016 | tf_op jit(solution)/shard_map/psum | solution.py:12
  92.5 2.5 fusion.18
  95.1 35.5 %all-reduce.29.cloned.1.call-done = (bf16[256,1000]{0,1:T(8,128)(2,1)}, bf16[256,1000]{0,1:T(8,128)(2,1)}) async-done(((bf16[256,1000]{0,1:T(8,128)(2,1)}, bf16[256,1000]{0,1:T(8,128)(2,1)}), (bf16[256,1000]{0,1:T(8,128)(2,1)}, bf16[256,1000]{0,1:T(8,128)(2,1)})) %all-reduce.29.cloned.1.call-update) | async-done | bytes 1024016 | tf_op jit(solution)/shard_map/psum | solution.py:8
  130.6 2.7 fusion.8
  133.3 2.5 fusion.11
  138.2 99.2 %all-reduce.23.cloned.1.call-done = (bf16[512,1000]{0,1:T(8,128)(2,1)}, bf16[512,1000]{0,1:T(8,128)(2,1)}) async-done(((bf16[512,1000]{0,1:T(8,128)(2,1)}, bf16[512,1000]{0,1:T(8,128)(2,1)}), (bf16[512,1000]{0,1:T(8,128)(2,1)}, bf16[512,1000]{0,1:T(8,128)(2,1)})) %all-reduce.23.cloned.1.call-update) | async-done | bytes 2048016 | tf_op jit(solution)/shard_map/psum | solution.py:12
  237.4 3.0 fusion.19
  242.6 35.8 %all-reduce.27.cloned.1.call-done = (bf16[256,1000]{0,1:T(8,128)(2,1)}, bf16[256,1000]{0,1:T(8,128)(2,1)}) async-done(((bf16[256,1000]{0,1:T(8,128)(2,1)}, bf16[256,1000]{0,1:T(8,128)(2,1)}), (bf16[256,1000]{0,1:T(8,128)(2,1)}, bf16[256,1000]{0,1:T(8,128)(2,1)})) %all-reduce.27.cloned.1.call-update) | async-done | bytes 1024016 | tf_op jit(solution)/shard_map/psum | solution.py:8
  282.5 2.5 fusion.9
  288.8 97.8 %all-reduce.21.cloned.1.call-done = (bf16[512,1000]{0,1:T(8,128)(2,1)}, bf16[512,1000]{0,1:T(8,128)(2,1)}) async-done(((bf16[512,1000]{0,1:T(8,128)(2,1)}, bf16[512,1000]{0,1:T(8,128)(2,1)}), (bf16[512,1000]{0,1:T(8,128)(2,1)}, bf16[512,1000]{0,1:T(8,128)(2,1)})) %all-reduce.21.cloned.1.call-update) | async-done | bytes 2048016 | tf_op jit(solution)/shard_map/psum | solution.py:12
  386.6 3.0 fusion.20
  391.9 2.7 fusion.49
  394.6 33.1 %all-reduce.25.cloned.1.call-done = (bf16[256,1000]{0,1:T(8,128)(2,1)}, bf16[256,1000]{0,1:T(8,128)(2,1)}) async-done(((bf16[256,1000]{0,1:T(8,128)(2,1)}, bf16[256,1000]{0,1:T(8,128)(2,1)}), (bf16[256,1000]{0,1:T(8,128)(2,1)}, bf16[256,1000]{0,1:T(8,128)(2,1)})) %all-reduce.25.cloned.1.call-update) | async-done | bytes 1024016 | tf_op jit(solution)/shard_map/psum | solution.py:8
  429.5 2.5 fusion.10
  434.5 101.6 %all-reduce.19.cloned.1.call-done = (bf16[1,512,1000]{1,2,0:T(8,128)(2,1)}, bf16[512,1000]{0,1:T(8,128)(2,1)}) async-done(((bf16[1,512,1000]{1,2,0:T(8,128)(2,1)}, bf16[512,1000]{0,1:T(8,128)(2,1)}), (bf16[1,512,1000]{1,2,0:T(8,128)(2,1)}, bf16[512,1000]{0,1:T(8,128)(2,1)})) %all-reduce.19.cloned.1.call-update) | async-done | bytes 2048016 | tf_op jit(solution)/shard_map/psum | solution.py:12
  536.0 2.8 fusion.21
  542.9 35.5 %fusion.4 = bf16[7168,1000]{0,1:T(8,128)(2,1)} fusion(bf16[4,512,1000]{1,2,0:T(8,128)(2,1)S(1)} %pad_maximum_fusion, bf16[4,512,7168]{2,1,0:T(8,128)(2,1)} %param.14), kind=kOutput, calls=%fused_computation.4 | convolution fusion | flops 29367296000 | bytes 47792128 | tf_op jit(solution)/shard_map/dot_general | solution.py:16
  580.2 38.3 %fusion.1 = bf16[14336,1000]{0,1:T(8,128)(2,1)} fusion(bf16[4,256,1000]{1,2,0:T(8,128)(2,1)S(1)} %pad_maximum_fusion.1, bf16[14336,4,256]{2,1,0:T(4,128)(2,1)} %param.19), kind=kOutput, calls=%fused_computation.3 | convolution fusion | flops 29374464000 | bytes 60080128 | tf_op jit(solution)/shard_map/dot_general | solution.py:88
  618.6 73.9 %reduce-scatter.3.cloned.1.call-done = bf16[1792,1000]{0,1:T(8,128)(2,1)} async-done(((bf16[7168,1000]{0,1:T(8,128)(2,1)}), bf16[1792,1000]{0,1:T(8,128)(2,1)}) %reduce-scatter.3.cloned.1.call-update) | async-done | bytes 3584016 | tf_op jit(solution)/shard_map/reduce_scatter | solution.py:59
  692.4 5.8 subtract_convert_fusion.1
  698.2 518.4 %reduce-scatter.5.cloned.1.call-done = bf16[1792,1000]{0,1:T(8,128)(2,1)} async-done(((bf16[14336,1000]{0,1:T(8,128)(2,1)}), bf16[1792,1000]{0,1:T(8,128)(2,1)}) %reduce-scatter.5.cloned.1.call-update) | async-done | bytes 3584016 | tf_op jit(solution)/shard_map/reduce_scatter | solution.py:87
  1216.7 5.8 subtract_convert_fusion
  (56 shorter events, 24.8 us)
Async XLA Ops:
  7.2 85.3 %all-reduce.15.cloned.1.call-start = ((), (), s32[]{:S(2)}) async-start(), calls=%async_computation.2 | async-start | bytes 2048000 | tf_op jit(solution)/shard_map/psum | solution.py:12
  9.7 120.8 %all-reduce.29.cloned.1.call-start = ((), (), s32[]{:S(2)}) async-start(), calls=%async_computation.11 | async-start | bytes 2048000 | tf_op jit(solution)/shard_map/psum | solution.py:8
  95.0 142.4 %all-reduce.23.cloned.1.call-start = ((), (), s32[]{:S(2)}) async-start(), calls=%async_computation.8 | async-start | bytes 4096000 | tf_op jit(solution)/shard_map/psum | solution.py:12
  130.6 2.7 copy-start.2
  133.3 2.5 copy-start
  135.8 142.7 %all-reduce.27.cloned.1.call-start = ((), (), s32[]{:S(2)}) async-start(), calls=%async_computation.10 | async-start | bytes 2048000 | tf_op jit(solution)/shard_map/psum | solution.py:8
  237.4 3.0 copy-start.1
  237.4 3.0 copy-start.8
  242.6 144.0 %all-reduce.21.cloned.1.call-start = ((), (), s32[]{:S(2)}) async-start(), calls=%async_computation.7 | async-start | bytes 4096000 | tf_op jit(solution)/shard_map/psum | solution.py:12
  280.0 2.4 copy-start.10
  285.0 142.8 %all-reduce.25.cloned.1.call-start = ((), (), s32[]{:S(2)}) async-start(), calls=%async_computation.9 | async-start | bytes 2048000 | tf_op jit(solution)/shard_map/psum | solution.py:8
  386.6 3.0 copy-start.6
  386.6 3.0 copy-start.7
  389.6 2.3 copy-start.4
  391.9 144.1 %all-reduce.19.cloned.1.call-start = ((), (), s32[]{:S(2)}) async-start(), calls=%async_computation.6 | async-start | bytes 4096000 | tf_op jit(solution)/shard_map/psum | solution.py:12
  427.8 1.7 copy-start.11
  427.8 4.2 copy-start.3
  434.4 144.3 %all-reduce.17.cloned.1.call-start = ((), (), s32[]{:S(2)}) async-start(), calls=%async_computation.4 | async-start | bytes 1024000 | tf_op jit(solution)/shard_map/psum | solution.py:8
  538.9 153.6 %reduce-scatter.3.cloned.1.call-start = ((), (), s32[]{:S(2)}) async-start(), calls=%async_computation.3 | async-start | bytes 17920000 | tf_op jit(solution)/shard_map/reduce_scatter | solution.py:59
  540.9 2.0 copy-start.5
  578.4 638.2 %reduce-scatter.5.cloned.1.call-start = ((), (), s32[]{:S(2)}) async-start(), calls=%async_computation.5 | async-start | bytes 32256000 | tf_op jit(solution)/shard_map/reduce_scatter | solution.py:87
  580.2 38.4 %copy-start.9 = (bf16[4,256,1000]{1,2,0:T(8,128)(2,1)}, bf16[4,256,1000]{1,2,0:T(8,128)(2,1)S(1)}, u32[]{:S(2)}) copy-start(bf16[4,256,1000]{1,2,0:T(8,128)(2,1)S(1)} %pad_maximum_fusion.1) | copy-start | bytes 6144004
Sparse Core Ops, SparseCore 0:
  12.1 80.3 all-reduce.14
  95.6 34.9 all-reduce.28
  135.9 101.4 all-reduce.22
  242.7 35.7 all-reduce.26
  285.1 101.4 all-reduce.20
  392.0 35.7 all-reduce.24
  434.5 101.4 all-reduce.18
  539.1 32.7 all-reduce.16
  578.6 113.8 reduce-scatter.2
  696.4 520.2 reduce-scatter.4
where the time goes:
time: 1230 us
  waiting for transfers between devices  1080 us (88%)
  matrix products  122 us (10%)
  other arithmetic  14.8 us (1%)
  between operations  14.3 us (1%)
    reduce_scatter x1, waiting for transfers between devices, local(): lax.psum_scatter(jnp.dot(flat_back, flat_upper, preferred_element_type=jn...  518 us
    psum x4, waiting for transfers between devices, reduce_col(): return lax.psum(value.astype(jnp.bfloat16), 'col').astype(jnp.float32)  379 us
    psum x4, waiting for transfers between devices, reduce_row(): return lax.psum(value.astype(jnp.bfloat16), 'row').astype(jnp.float32)  104 us
    reduce_scatter x1, waiting for transfers between devices, local(): lax.psum_scatter(leading_dot(flat_slab, flat_lower).astype(jnp.bfloat16),...  73.9 us
    dot_general x11, matrix products, leading_dot(): lax.dot_general(left, right, (((0,), (0,)), ((), ())), preferred_element_...  58.7 us
    dot_general x1, matrix products, local(): jnp.dot(flat_back, flat_upper, preferred_element_type=jnp.float32)  38.3 us
  transfers between devices with their start and end apart: 10, of which 9 were waited for; matrix products, arithmetic and copies ran while one was open for 8% of the time, Pallas kernels for 0%

commit v1 on v0

--- a/solution.py
+++ b/solution.py
@@ -1,7 +1,154 @@
+import functools
+
 import jax
 import jax.numpy as jnp
 from jax import lax
+from jax.experimental import pallas as pl
+from jax.experimental.pallas import tpu as pltpu
 from jax.sharding import PartitionSpec as P
+
+NZ = 4
+MESH = pl.DeviceIdType.MESH
+
+
+def add_rows(dst, src, rows, step):
+    def body(i, carry):
+        at = pl.ds(pl.multiple_of(i * step, step), step)
+        dst[at, :] = (dst[at, :].astype(jnp.float32) + src[at, :].astype(jnp.float32)).astype(
+            jnp.bfloat16
+        )
+        return carry
+
+    lax.fori_loop(0, rows // step, body, 0)
+
+
+def col_scatter_kernel(
+    nx, chunk, part, tail, out, from_x, from_z, own, x_send, x_recv, z_send, z_recv, own_sem
+):
+    rows = tail.shape[0]
+    count = rows // chunk
+    col = lax.axis_index("col")
+    z, x = col // nx, col % nx
+    step = 64
+
+    barrier = pltpu.get_barrier_semaphore()
+    for i in range(1, nx):
+        pl.semaphore_signal(
+            barrier, inc=1, device_id={"col": z * nx + (x + i) % nx}, device_id_type=MESH
+        )
+    for j in range(1, NZ):
+        pl.semaphore_signal(
+            barrier, inc=1, device_id={"col": (z + j) % NZ * nx + x}, device_id_type=MESH
+        )
+    pl.semaphore_wait(barrier, nx - 1 + NZ - 1)
+
+    units = [(k, j) for k in range(count) for j in range(NZ)]
+
+    def piece(k, j, to_x):
+        return part.at[pl.ds(pl.multiple_of(((z + 1 + j) % NZ * nx + to_x) * rows + k * chunk, 64), chunk), :]
+
+    def x_copy(u, i):
+        k, j = units[u]
+        to_x = (x + i) % nx
+        return pltpu.make_async_remote_copy(
+            src_ref=piece(k, j, to_x),
+            dst_ref=from_x.at[i - 1, u],
+            send_sem=x_send.at[i - 1, u],
+            recv_sem=x_recv.at[i - 1, u],
+            device_id={"col": z * nx + to_x},
+            device_id_type=MESH,
+        )
+
+    def own_copy(u):
+        k, j = units[u]
+        return pltpu.make_async_copy(piece(k, j, x), own.at[u % 2], own_sem.at[u % 2])
+
+    def z_copy(u):
+        k, j = units[u]
+        return pltpu.make_async_remote_copy(
+            src_ref=from_x.at[0, u],
+            dst_ref=from_z.at[j, k],
+            send_sem=z_send.at[j, k],
+            recv_sem=z_recv.at[j, k],
+            device_id={"col": (z + 1 + j) % NZ * nx + x},
+            device_id_type=MESH,
+        )
+
+    ahead = 4
+    for u in range(min(ahead, len(units))):
+        for i in range(1, nx):
+            x_copy(u, i).start()
+    own_copy(0).start()
+
+    def finish(k):
+        for j in range(NZ - 1):
+            z_copy(k * NZ + j).wait_recv()
+        mine = from_x.at[0, k * NZ + NZ - 1]
+
+        def body(i, carry):
+            at = pl.ds(pl.multiple_of(i * step, step), step)
+            total = mine[at, :].astype(jnp.float32)
+            for j in range(NZ - 1):
+                total = total + from_z[j, k, at, :].astype(jnp.float32)
+            here = pl.ds(pl.multiple_of(k * chunk + i * step, step), step)
+            out[here, :] = (tail[here, :].astype(jnp.float32) - total).astype(jnp.bfloat16)
+            return carry
+
+        lax.fori_loop(0, chunk // step, body, 0)
+
+    for u, (k, j) in enumerate(units):
+        if u + 1 < len(units):
+            own_copy(u + 1).start()
+        own_copy(u).wait()
+        for i in range(1, nx):
+            x_copy(u, i).wait_recv()
+        if u + ahead < len(units):
+            for i in range(1, nx):
+                x_copy(u + ahead, i).start()
+        add_rows(from_x.at[0, u], own.at[u % 2], chunk, step)
+        for i in range(2, nx):
+            add_rows(from_x.at[0, u], from_x.at[i - 1, u], chunk, step)
+        if j < NZ - 1:
+            z_copy(u).start()
+        elif k >= 1:
+            finish(k - 1)
+    finish(count - 1)
+    for u, (k, j) in enumerate(units):
+        for i in range(1, nx):
+            x_copy(u, i).wait_send()
+        if j < NZ - 1:
+            z_copy(u).wait_send()
+
+
+def col_scatter(part, tail, ncol):
+    nx = ncol // NZ
+    rows, classes = tail.shape
+    chunk = 448
+    count = rows // chunk
+    vmem = pl.BlockSpec(memory_space=pltpu.VMEM)
+    return pl.pallas_call(
+        functools.partial(col_scatter_kernel, nx, chunk),
+        out_shape=jax.ShapeDtypeStruct(tail.shape, jnp.bfloat16),
+        in_specs=[pl.BlockSpec(memory_space=pl.ANY), vmem],
+        out_specs=vmem,
+        scratch_shapes=[
+            pltpu.VMEM((nx - 1, count * NZ, chunk, classes), jnp.bfloat16),
+            pltpu.VMEM((NZ - 1, count, chunk, classes), jnp.bfloat16),
+            pltpu.VMEM((2, chunk, classes), jnp.bfloat16),
+            pltpu.SemaphoreType.DMA((nx - 1, count * NZ)),
+            pltpu.SemaphoreType.DMA((nx - 1, count * NZ)),
+            pltpu.SemaphoreType.DMA((NZ - 1, count)),
+            pltpu.SemaphoreType.DMA((NZ - 1, count)),
+            pltpu.SemaphoreType.DMA((2,)),
+        ],
+        compiler_params=pltpu.CompilerParams(
+            collective_id=1, has_side_effects=True, vmem_limit_bytes=50 * 1024 * 1024
+        ),
+        cost_estimate=pl.CostEstimate(
+            flops=10**9, bytes_accessed=part.size * 16, transcendentals=0
+        ),
+        name="col_scatter",
+    )(part, tail)
 
 
 def reduce_row(value):
@@ -84,13 +231,8 @@
     panel_cols = upper_head.shape[1]
     flat_back = backward_slab.reshape(backward_slab.shape[0], panels * panel_cols)
     flat_upper = upper_head.reshape(panels * panel_cols, classes)
-    upper_update = lax.psum_scatter(
-        jnp.dot(flat_back, flat_upper, preferred_element_type=jnp.float32).astype(jnp.bfloat16),
-        "col",
-        scatter_dimension=0,
-        tiled=True,
-    ).astype(jnp.float32)
-    upper_tail = (backward_tail.astype(jnp.float32) - upper_update).astype(jnp.bfloat16)
+    part = jnp.dot(flat_back, flat_upper, preferred_element_type=jnp.float32).astype(jnp.bfloat16)
+    upper_tail = col_scatter(part, backward_tail, lax.axis_size("col"))
     return (lower_head, lower_tail, upper_head, upper_tail)
 
 

time: 1230 us -> 1030 us (0.84)
  waiting for transfers between devices: 1080 us -> 483 us
  Pallas kernels: 0 us -> 342 us
  local copies, waits for them, and re-layouts: 2.02 us -> 51.3 us
    reduce_scatter x1 -> x0, waiting for transfers between devices: 518 us -> none  [local(): lax.psum_scatter(jnp.dot(flat_back, flat_upper, preferred_element_type=jn...]
    pallas_call x0 -> x1, Pallas kernels: none -> 342 us  [col_scatter(): pl.pallas_call(functools.partial(col_scatter_kernel, nx, chunk), out_shap...]
    reduce_scatter x1, waiting for transfers between devices: 73.9 us -> 0.01 us  [local(): lax.psum_scatter(leading_dot(flat_slab, flat_lower).astype(jnp.bfloat16),...]
    convert_element_type x0 -> x1, local copies, waits for them, and re-layouts: none -> 35.5 us  [local(): jnp.dot(flat_back, flat_upper, preferred_element_type=jnp.float32)]
    unnamed x24 -> x28, local copies, waits for them, and re-layouts: 2.02 us -> 15.7 us
  transfers between devices with their start and end apart: 10 -> 9, of which waited for: 9 -> 7; matrix products, arithmetic and copies ran while one was open for 8% -> 13% of each run, Pallas kernels for 0% -> 33%
where the time goes in v1:
time: 1030 us; the launch traced here: 1020 us
  waiting for transfers between devices  483 us (47%)
  Pallas kernels  342 us (33%)
  matrix products  123 us (12%)
  local copies, waits for them, and re-layouts  51.3 us (5%)
  between operations  14 us (1%)
    psum x4, waiting for transfers between devices, reduce_col(): return lax.psum(value.astype(jnp.bfloat16), 'col').astype(jnp.float32)  379 us
    pallas_call x1, Pallas kernels, col_scatter(): pl.pallas_call(functools.partial(col_scatter_kernel, nx, chunk), out_shap...  342 us
    psum x4, waiting for transfers between devices, reduce_row(): return lax.psum(value.astype(jnp.bfloat16), 'row').astype(jnp.float32)  104 us
    dot_general x11, matrix products, leading_dot(): lax.dot_general(left, right, (((0,), (0,)), ((), ())), preferred_element_...  58.7 us
    dot_general x1, matrix products, local(): jnp.dot(flat_back, flat_upper, preferred_element_type=jnp.float32)  39.5 us
    convert_element_type x1, local copies, waits for them, and re-layouts, local(): jnp.dot(flat_back, flat_upper, preferred_element_type=jnp.float32)  35.5 us
  transfers between devices with their start and end apart: 9, of which 7 were waited for; matrix products, arithmetic and copies ran while one was open for 13% of the time, Pallas kernels for 33%

profile of v1, /device:TPU:0, one launch (start us, length us, event | category | flops | bytes accessed | tf_op | source)
XLA Modules:
  0.0 1023.5 jit_solution(2059557863219287177)
XLA Ops:
  7.2 2.5 convolution_convert_fusion.4
  9.8 2.6 convolution_convert_fusion.8
  12.4 80.2 %all-reduce.15.cloned.1.call-done = bf16[512,1000]{0,1:T(8,128)(2,1)} async-done(((bf16[512,1000]{0,1:T(8,128)(2,1)}), bf16[512,1000]{0,1:T(8,128)(2,1)}) %all-reduce.15.cloned.1.call-update) | async-done | bytes 1024016 | tf_op jit(solution)/shard_map/psum | solution.py:159
  92.5 2.5 fusion.15
  95.1 35.5 %all-reduce.29.cloned.1.call-done = (bf16[256,1000]{0,1:T(8,128)(2,1)}, bf16[256,1000]{0,1:T(8,128)(2,1)}) async-done(((bf16[256,1000]{0,1:T(8,128)(2,1)}, bf16[256,1000]{0,1:T(8,128)(2,1)}), (bf16[256,1000]{0,1:T(8,128)(2,1)}, bf16[256,1000]{0,1:T(8,128)(2,1)})) %all-reduce.29.cloned.1.call-update) | async-done | bytes 1024016 | tf_op jit(solution)/shard_map/psum | solution.py:155
  130.6 2.7 fusion.5
  138.2 99.2 %all-reduce.23.cloned.1.call-done = (bf16[512,1000]{0,1:T(8,128)(2,1)}, bf16[512,1000]{0,1:T(8,128)(2,1)}) async-done(((bf16[512,1000]{0,1:T(8,128)(2,1)}, bf16[512,1000]{0,1:T(8,128)(2,1)}), (bf16[512,1000]{0,1:T(8,128)(2,1)}, bf16[512,1000]{0,1:T(8,128)(2,1)})) %all-reduce.23.cloned.1.call-update) | async-done | bytes 2048016 | tf_op jit(solution)/shard_map/psum | solution.py:159
  237.4 3.0 fusion.16
  242.6 35.8 %all-reduce.27.cloned.1.call-done = (bf16[256,1000]{0,1:T(8,128)(2,1)}, bf16[256,1000]{0,1:T(8,128)(2,1)}) async-done(((bf16[256,1000]{0,1:T(8,128)(2,1)}, bf16[256,1000]{0,1:T(8,128)(2,1)}), (bf16[256,1000]{0,1:T(8,128)(2,1)}, bf16[256,1000]{0,1:T(8,128)(2,1)})) %all-reduce.27.cloned.1.call-update) | async-done | bytes 1024016 | tf_op jit(solution)/shard_map/psum | solution.py:155
  282.5 2.5 fusion.6
  288.8 97.8 %all-reduce.21.cloned.1.call-done = (bf16[512,1000]{0,1:T(8,128)(2,1)}, bf16[512,1000]{0,1:T(8,128)(2,1)}) async-done(((bf16[512,1000]{0,1:T(8,128)(2,1)}, bf16[512,1000]{0,1:T(8,128)(2,1)}), (bf16[512,1000]{0,1:T(8,128)(2,1)}, bf16[512,1000]{0,1:T(8,128)(2,1)})) %all-reduce.21.cloned.1.call-update) | async-done | bytes 2048016 | tf_op jit(solution)/shard_map/psum | solution.py:159
  386.6 3.0 fusion.17
  391.9 2.7 fusion.46
  394.6 33.1 %all-reduce.25.cloned.1.call-done = (bf16[256,1000]{0,1:T(8,128)(2,1)}, bf16[256,1000]{0,1:T(8,128)(2,1)}) async-done(((bf16[256,1000]{0,1:T(8,128)(2,1)}, bf16[256,1000]{0,1:T(8,128)(2,1)}), (bf16[256,1000]{0,1:T(8,128)(2,1)}, bf16[256,1000]{0,1:T(8,128)(2,1)})) %all-reduce.25.cloned.1.call-update) | async-done | bytes 1024016 | tf_op jit(solution)/shard_map/psum | solution.py:155
  429.5 2.5 fusion.7
  434.5 101.6 %all-reduce.19.cloned.1.call-done = (bf16[1,512,1000]{1,2,0:T(8,128)(2,1)}, bf16[512,1000]{0,1:T(8,128)(2,1)}) async-done(((bf16[1,512,1000]{1,2,0:T(8,128)(2,1)}, bf16[512,1000]{0,1:T(8,128)(2,1)}), (bf16[1,512,1000]{1,2,0:T(8,128)(2,1)}, bf16[512,1000]{0,1:T(8,128)(2,1)})) %all-reduce.19.cloned.1.call-update) | async-done | bytes 2048016 | tf_op jit(solution)/shard_map/psum | solution.py:159
  536.0 2.8 fusion.18
  542.9 35.5 %fusion.1 = bf16[7168,1000]{0,1:T(8,128)(2,1)} fusion(bf16[4,512,1000]{1,2,0:T(8,128)(2,1)S(1)} %pad_maximum_fusion, bf16[4,512,7168]{2,1,0:T(8,128)(2,1)} %param.14), kind=kOutput, calls=%fused_computation.3 | convolution fusion | flops 29367296000 | bytes 47792128 | tf_op jit(solution)/shard_map/dot_general | solution.py:163
  578.4 6.0 copy.20.tail
  585.9 39.5 %bitcast_convert_fusion = bf16[1000,14336]{1,0:T(8,128)(2,1)} fusion(bf16[4,256,1000]{1,2,0:T(8,128)(2,1)S(1)} %pad_maximum_fusion.1, bf16[14336,4,256]{2,1,0:T(4,128)(2,1)} %param.19), kind=kOutput, calls=%fused_computation | convolution fusion | flops 29374464000 | bytes 60080128 | tf_op jit(solution)/shard_map/dot_general | solution.py:234
  625.4 35.5 %copy.19 = bf16[1000,14336]{0,1:T(8,128)(2,1)} copy(bf16[1000,14336]{1,0:T(8,128)(2,1)} %bitcast_convert_fusion) | data formatting | bytes 57344000 | tf_op jit(solution)/shard_map/convert_element_type | solution.py:234
  660.9 342.5 %col_scatter.1 = bf16[1792,1000]{1,0:T(8,128)(2,1)S(1)} custom-call(bf16[14336,1000]{1,0:T(8,128)(2,1)} %bitcast.160, bf16[1792,1000]{1,0:T(8,128)(2,1)} %copy.20.tail), custom_call_target="tpu_custom_call" | custom-call | flops 1000000000 | bytes 229376000 | tf_op jit(solution)/shard_map/col_scatter/pallas_call | solution.py:129
  1005.2 6.0 copy.21
  1011.2 5.8 subtract_convert_fusion
  (58 shorter events, 28.8 us)
Async XLA Ops:
  7.2 85.3 %all-reduce.15.cloned.1.call-start = ((), (), s32[]{:S(2)}) async-start(), calls=%async_computation.1 | async-start | bytes 2048000 | tf_op jit(solution)/shard_map/psum | solution.py:159
  9.7 120.8 %all-reduce.29.cloned.1.call-start = ((), (), s32[]{:S(2)}) async-start(), calls=%async_computation.9 | async-start | bytes 2048000 | tf_op jit(solution)/shard_map/psum | solution.py:155
  95.0 142.4 %all-reduce.23.cloned.1.call-start = ((), (), s32[]{:S(2)}) async-start(), calls=%async_computation.6 | async-start | bytes 4096000 | tf_op jit(solution)/shard_map/psum | solution.py:159
  130.6 2.7 copy-start.3
  133.3 2.5 copy-start.1
  135.8 142.7 %all-reduce.27.cloned.1.call-start = ((), (), s32[]{:S(2)}) async-start(), calls=%async_computation.8 | async-start | bytes 2048000 | tf_op jit(solution)/shard_map/psum | solution.py:155
  237.4 3.0 copy-start.2
  237.4 3.0 copy-start.9
  242.6 144.0 %all-reduce.21.cloned.1.call-start = ((), (), s32[]{:S(2)}) async-start(), calls=%async_computation.5 | async-start | bytes 4096000 | tf_op jit(solution)/shard_map/psum | solution.py:159
  280.0 2.4 copy-start.11
  285.0 142.8 %all-reduce.25.cloned.1.call-start = ((), (), s32[]{:S(2)}) async-start(), calls=%async_computation.7 | async-start | bytes 2048000 | tf_op jit(solution)/shard_map/psum | solution.py:155
  386.6 3.0 copy-start.7
  386.6 3.0 copy-start.8
  389.6 2.3 copy-start.5
  391.9 144.1 %all-reduce.19.cloned.1.call-start = ((), (), s32[]{:S(2)}) async-start(), calls=%async_computation.4 | async-start | bytes 4096000 | tf_op jit(solution)/shard_map/psum | solution.py:159
  427.8 1.7 copy-start.12
  427.8 4.2 copy-start.4
  434.4 150.0 %all-reduce.17.cloned.1.call-start = ((), (), s32[]{:S(2)}) async-start(), calls=%async_computation.3 | async-start | bytes 1024000 | tf_op jit(solution)/shard_map/psum | solution.py:155
  538.9 472.3 %reduce-scatter.2.cloned.1.call-start = ((), (), s32[]{:S(2)}) async-start(), calls=%async_computation.2 | async-start | bytes 17920000 | tf_op jit(solution)/shard_map/reduce_scatter | solution.py:206
  540.9 2.0 copy-start.6
  585.9 39.5 %copy-start.10 = (bf16[4,256,1000]{1,2,0:T(8,128)(2,1)}, bf16[4,256,1000]{1,2,0:T(8,128)(2,1)S(1)}, u32[]{:S(2)}) copy-start(bf16[4,256,1000]{1,2,0:T(8,128)(2,1)S(1)} %pad_maximum_fusion.1) | copy-start | bytes 6144004
  1003.4 1.8 copy-start
Sparse Core Ops, SparseCore 0:
  12.1 80.3 all-reduce.14
  95.6 34.9 all-reduce.28
  135.9 101.4 all-reduce.22
  242.7 35.7 all-reduce.26
  285.1 101.4 all-reduce.20
  392.0 35.7 all-reduce.24
  434.5 101.4 all-reduce.18
  539.1 32.7 all-reduce.16
  578.5 113.8 reduce-scatter.1

commit v2 on v1

--- a/solution.py
+++ b/solution.py
@@ -151,12 +151,149 @@
     )(part, tail)
 
 
+def col_reduce_kernel(
+    nx, value, out, from_x, from_z, full, x_send, x_recv, z_send, z_recv, gx_send, gx_recv, gz_send, gz_recv
+):
+    rows = full.shape[1]
+    col = lax.axis_index("col")
+    z, x = col // nx, col % nx
+    step = 16
+
+    barrier = pltpu.get_barrier_semaphore()
+    for i in range(1, nx):
+        pl.semaphore_signal(
+            barrier, inc=1, device_id={"col": z * nx + (x + i) % nx}, device_id_type=MESH
+        )
+    for j in range(1, NZ):
+        pl.semaphore_signal(
+            barrier, inc=1, device_id={"col": (z + j) % NZ * nx + x}, device_id_type=MESH
+        )
+    pl.semaphore_wait(barrier, nx - 1 + NZ - 1)
+
+    def piece(j, to_x):
+        start = ((z + 1 + j) % NZ * nx + to_x) * rows
+        return value.at[pl.ds(pl.multiple_of(start, 16), rows), :]
+
+    def remote(src, dst, send, recv, target):
+        return pltpu.make_async_remote_copy(
+            src_ref=src,
+            dst_ref=dst,
+            send_sem=send,
+            recv_sem=recv,
+            device_id={"col": target},
+            device_id_type=MESH,
+        )
+
+    def x_copy(j, i):
+        to_x = (x + i) % nx
+        return remote(
+            piece(j, to_x), from_x.at[i - 1, j], x_send.at[i - 1, j], x_recv.at[i - 1, j], z * nx + to_x
+        )
+
+    def z_copy(j):
+        return remote(
+            from_x.at[0, j], from_z.at[j], z_send.at[j], z_recv.at[j], (z + 1 + j) % NZ * nx + x
+        )
+
+    def gather_z(j):
+        return remote(
+            full.at[col], full.at[col], gz_send.at[j], gz_recv.at[j], (z + 1 + j) % NZ * nx + x
+        )
+
+    def gather_x(j, i, of_x):
+        block = full.at[(z + NZ - 1 - j) % NZ * nx + of_x]
+        return remote(
+            block, block, gx_send.at[i - 1, j], gx_recv.at[i - 1, j], z * nx + (x + i) % nx
+        )
+
+    for j in range(NZ):
+        for i in range(1, nx):
+            x_copy(j, i).start()
+    for j in range(NZ):
+        for i in range(1, nx):
+            x_copy(j, i).wait_recv()
+        add_rows(from_x.at[0, j], piece(j, x), rows, step)
+        for i in range(2, nx):
+            add_rows(from_x.at[0, j], from_x.at[i - 1, j], rows, step)
+        if j < NZ - 1:
+            z_copy(j).start()
+    for j in range(NZ - 1):
+        z_copy(j).wait_recv()
+
+    def body(i, carry):
+        at = pl.ds(pl.multiple_of(i * step, step), step)
+        total = from_x[0, NZ - 1, at, :].astype(jnp.float32)
+        for j in range(NZ - 1):
+            total = total + from_z[j, at, :].astype(jnp.float32)
+        full[col, at, :] = total.astype(jnp.bfloat16)
+        return carry
+
+    lax.fori_loop(0, rows // step, body, 0)
+    for j in range(NZ - 1):
+        gather_z(j).start()
+    for i in range(1, nx):
+        gather_x(NZ - 1, i, x).start()
+    for j in range(NZ - 1):
+        block = full.at[(z + NZ - 1 - j) % NZ * nx + x]
+        remote(
+            block, block, gz_send.at[j], gz_recv.at[j], (z + 1 + j) % NZ * nx + x
+        ).wait_recv()
+        for i in range(1, nx):
+            gather_x(j, i, x).start()
+    for j in range(NZ):
+        for i in range(1, nx):
+            gather_x(j, i, (x + nx - i) % nx).wait_recv()
+    for j in range(NZ):
+        for i in range(1, nx):
+            x_copy(j, i).wait_send()
+            gather_x(j, i, x).wait_send()
+        if j < NZ - 1:
+            z_copy(j).wait_send()
+            gather_z(j).wait_send()
+
+    def emit(b, carry):
+        out[pl.ds(pl.multiple_of(b * rows, 16), rows), :] = full[b]
+        return carry
+
+    lax.fori_loop(0, full.shape[0], emit, 0)
+
+
+def col_reduce(value, ident):
+    ncol = lax.axis_size("col")
+    nx = ncol // NZ
+    rows, classes = value.shape[0] // ncol, value.shape[1]
+    vmem = pl.BlockSpec(memory_space=pltpu.VMEM)
+    dma = pltpu.SemaphoreType.DMA
+    return pl.pallas_call(
+        functools.partial(col_reduce_kernel, nx),
+        out_shape=jax.ShapeDtypeStruct(value.shape, jnp.bfloat16),
+        in_specs=[vmem],
+        out_specs=vmem,
+        scratch_shapes=[
+            pltpu.VMEM((nx - 1, NZ, rows, classes), jnp.bfloat16),
+            pltpu.VMEM((NZ - 1, rows, classes), jnp.bfloat16),
+            pltpu.VMEM((ncol, rows, classes), jnp.bfloat16),
+            dma((nx - 1, NZ)),
+            dma((nx - 1, NZ)),
+            dma((NZ - 1,)),
+            dma((NZ - 1,)),
+            dma((nx - 1, NZ)),
+            dma((nx - 1, NZ)),
+            dma((NZ - 1,)),
+            dma((NZ - 1,)),
+        ],
+        compiler_params=pltpu.CompilerParams(
+            collective_id=ident, has_side_effects=True, vmem_limit_bytes=24 * 1024 * 1024
+        ),
+        cost_estimate=pl.CostEstimate(
+            flops=10**7, bytes_accessed=value.size * 16, transcendentals=0
+        ),
+        name="col_reduce",
+    )(value)
+
+
 def reduce_row(value):
     return lax.psum(value.astype(jnp.bfloat16), "row").astype(jnp.float32)
-
-
-def reduce_col(value):
-    return lax.psum(value.astype(jnp.bfloat16), "col").astype(jnp.float32)
 
 
 def leading_dot(left, right):
@@ -179,26 +316,37 @@
 ):
     classes = forward_head.shape[2]
     panels = forward_head.shape[0]
-    lower_list = []
-    for panel_index in range(panels):
-        if panel_index == 0:
-            adjusted = forward_head[0]
-        else:
-            summed = leading_dot(
-                forward_coupling[panel_index * (panel_index - 1) // 2], lower_list[0]
+    bf16, f32 = jnp.bfloat16, jnp.float32
+    last = panels - 1
+    lower_list = [col_reduce(leading_dot(forward_inverse[0], forward_head[0]).astype(bf16), 2)]
+    upper_list = [None] * panels
+    upper_list[last] = reduce_row(
+        jnp.dot(backward_inverse[last], backward_head[last], preferred_element_type=f32)
+    ).astype(bf16)
+    for stage in range(1, panels):
+        summed = None
+        for earlier in range(stage):
+            product = leading_dot(
+                forward_coupling[stage * (stage - 1) // 2 + earlier], lower_list[earlier]
             )
-            for earlier in range(1, panel_index):
-                summed = summed + leading_dot(
-                    forward_coupling[panel_index * (panel_index - 1) // 2 + earlier],
-                    lower_list[earlier],
-                )
-            coupling = reduce_row(summed)
-            adjusted = (forward_head[panel_index].astype(jnp.float32) - coupling).astype(
-                jnp.bfloat16
+            summed = product if summed is None else summed + product
+        adjusted = (forward_head[stage].astype(f32) - reduce_row(summed)).astype(bf16)
+        back = last - stage
+        pulled = None
+        for later in range(back + 1, panels):
+            product = jnp.dot(
+                backward_coupling[later * (later - 1) // 2 + back],
+                upper_list[later],
+                preferred_element_type=f32,
             )
-        lower_list.append(
-            reduce_col(leading_dot(forward_inverse[panel_index], adjusted)).astype(jnp.bfloat16)
-        )
+            pulled = product if pulled is None else pulled + product
+        lower = leading_dot(forward_inverse[stage], adjusted).astype(bf16)
+        both = col_reduce(jnp.concatenate([lower, pulled.astype(bf16)]), 3)
+        lower_list.append(both[: lower.shape[0]])
+        shifted = (backward_head[back].astype(f32) - both[lower.shape[0] :].astype(f32)).astype(bf16)
+        upper_list[back] = reduce_row(
+            jnp.dot(backward_inverse[back], shifted, preferred_element_type=f32)
+        ).astype(bf16)
     lower_head = jnp.stack(lower_list)
     panel_rows = lower_head.shape[1]
     flat_lower = lower_head.reshape(panels * panel_rows, classes)
@@ -210,23 +358,6 @@
         tiled=True,
     ).astype(jnp.float32)
     lower_tail = (forward_tail.astype(jnp.float32) - lower_update).astype(jnp.bfloat16)
-    upper_list = [None] * panels
-    for panel_index in reversed(range(panels)):
-        if panel_index == panels - 1:
-            shifted = backward_head[panel_index]
-        else:
-            summed = None
-            for later_panel in range(panel_index + 1, panels):
-                block = backward_coupling[later_panel * (later_panel - 1) // 2 + panel_index]
-                product = jnp.dot(
-                    block, upper_list[later_panel], preferred_element_type=jnp.float32
-                )
-                summed = product if summed is None else summed + product
-            pulled = reduce_col(summed)
-            shifted = (backward_head[panel_index].astype(jnp.float32) - pulled).astype(jnp.bfloat16)
-        upper_list[panel_index] = reduce_row(
-            jnp.dot(backward_inverse[panel_index], shifted, preferred_element_type=jnp.float32)
-        ).astype(jnp.bfloat16)
     upper_head = jnp.stack(upper_list)
     panel_cols = upper_head.shape[1]
     flat_back = backward_slab.reshape(backward_slab.shape[0], panels * panel_cols)

time: 1030 us -> 917 us (0.89)
  waiting for transfers between devices: 483 us -> 106 us
  Pallas kernels: 342 us -> 578 us
  local copies, waits for them, and re-layouts: 51.3 us -> 81.5 us
    psum x4 -> x0, waiting for transfers between devices: 379 us -> none  [reduce_col(): return lax.psum(value.astype(jnp.bfloat16), 'col').astype(jnp.float32)]
    pallas_call x0 -> x4, Pallas kernels: none -> 232 us  [col_reduce(): pl.pallas_call(functools.partial(col_reduce_kernel, nx), out_shape=jax.Sh...]
    unnamed x28 -> x40, local copies, waits for them, and re-layouts: 15.7 us -> 26.4 us
  transfers between devices with their start and end apart: 9 -> 5, of which waited for: 7 -> 3; matrix products, arithmetic and copies ran while one was open for 13% -> 17% of each run, Pallas kernels for 33% -> 38%
where the time goes in v2:
time: 917 us; the launch traced here: 914 us
  Pallas kernels  578 us (63%)
  matrix products  121 us (13%)
  waiting for transfers between devices  106 us (12%)
  local copies, waits for them, and re-layouts  81.5 us (9%)
  between operations  14.1 us (2%)
  other arithmetic  13.2 us (1%)
    pallas_call x1, Pallas kernels, col_scatter(): pl.pallas_call(functools.partial(col_scatter_kernel, nx, chunk), out_shap...  346 us
    pallas_call x4, Pallas kernels, col_reduce(): pl.pallas_call(functools.partial(col_reduce_kernel, nx), out_shape=jax.Sh...  232 us
    psum x4, waiting for transfers between devices, reduce_row(): return lax.psum(value.astype(jnp.bfloat16), 'row').astype(jnp.float32)  106 us
    dot_general x11, matrix products, leading_dot(): lax.dot_general(left, right, (((0,), (0,)), ((), ())), preferred_element_...  59.5 us
    dot_general x1, matrix products, local(): jnp.dot(flat_back, flat_upper, preferred_element_type=jnp.float32)  39.5 us
    convert_element_type x1, local copies, waits for them, and re-layouts, local(): jnp.dot(flat_back, flat_upper, preferred_element_type=jnp.float32)  38.4 us
    unnamed x40, local copies, waits for them, and re-layouts  26.4 us
  transfers between devices with their start and end apart: 5, of which 3 were waited for; matrix products, arithmetic and copies ran while one was open for 17% of the time, Pallas kernels for 38%

profile of v2, /device:TPU:0, one launch (start us, length us, event | category | flops | bytes accessed | tf_op | source)
XLA Modules:
  0.0 914.1 jit_solution(4588685325027004808)
XLA Ops:
  9.3 38.0 %col_reduce.4 = bf16[512,1000]{1,0:T(8,128)(2,1)S(1)} custom-call(bf16[512,1000]{1,0:T(8,128)(2,1)S(1)} %copy.33.value), custom_call_target="tpu_custom_call" | custom-call | flops 10000000 | bytes 8192000 | tf_op jit(solution)/shard_map/col_reduce/pallas_call | solution.py:267
  49.5 2.5 convolution_convert_fusion.8
  52.1 3.1 fusion.86
  62.5 30.1 %all-reduce.14.cloned.1.call-done = (bf16[256,1000]{0,1:T(8,128)(2,1)}, bf16[256,1000]{0,1:T(8,128)(2,1)}) async-done(((bf16[256,1000]{0,1:T(8,128)(2,1)}, bf16[256,1000]{0,1:T(8,128)(2,1)}), (bf16[256,1000]{0,1:T(8,128)(2,1)}, bf16[256,1000]{0,1:T(8,128)(2,1)})) %all-reduce.14.cloned.1.call-update) | async-done | bytes 1024016 | tf_op jit(solution)/shard_map/psum | solution.py:296
  94.7 2.7 convolution_convert_fusion.3
  99.1 64.8 %col_reduce.5 = bf16[1024,1000]{1,0:T(8,128)(2,1)S(1)} custom-call(bf16[1024,1000]{1,0:T(8,128)(2,1)S(1)} %pad_maximum_fusion.1.value), custom_call_target="tpu_custom_call" | custom-call | flops 10000000 | bytes 16384000 | tf_op jit(solution)/shard_map/col_reduce/pallas_call | solution.py:267
  172.5 37.5 %all-reduce.12.cloned.1.call-done = (bf16[256,1000]{0,1:T(8,128)(2,1)}, bf16[256,1000]{0,1:T(8,128)(2,1)}) async-done(((bf16[256,1000]{0,1:T(8,128)(2,1)}, bf16[256,1000]{0,1:T(8,128)(2,1)}), (bf16[256,1000]{0,1:T(8,128)(2,1)}, bf16[256,1000]{0,1:T(8,128)(2,1)})) %all-reduce.12.cloned.1.call-update) | async-done | bytes 1024016 | tf_op jit(solution)/shard_map/psum | solution.py:296
  216.3 2.7 convolution_convert_fusion.1
  223.1 64.8 %col_reduce.6 = bf16[1024,1000]{1,0:T(8,128)(2,1)S(1)} custom-call(bf16[1024,1000]{1,0:T(8,128)(2,1)S(1)} %pad_maximum_fusion.2.value), custom_call_target="tpu_custom_call" | custom-call | flops 10000000 | bytes 16384000 | tf_op jit(solution)/shard_map/col_reduce/pallas_call | solution.py:267
  288.0 2.5 fusion.8
  296.1 38.1 %all-reduce.10.cloned.1.call-done = (bf16[256,1000]{0,1:T(8,128)(2,1)}, bf16[256,1000]{0,1:T(8,128)(2,1)}) async-done(((bf16[256,1000]{0,1:T(8,128)(2,1)}, bf16[256,1000]{0,1:T(8,128)(2,1)}), (bf16[256,1000]{0,1:T(8,128)(2,1)}, bf16[256,1000]{0,1:T(8,128)(2,1)})) %all-reduce.10.cloned.1.call-update) | async-done | bytes 1024016 | tf_op jit(solution)/shard_map/psum | solution.py:296
  335.8 2.7 convolution_add_fusion
  340.5 2.6 fusion.5
  343.1 2.6 convolution_convert_fusion
  347.5 64.8 %col_reduce.7 = bf16[1024,1000]{1,0:T(8,128)(2,1)S(1)} custom-call(bf16[1024,1000]{1,0:T(8,128)(2,1)S(1)} %pad_maximum_fusion.3.value), custom_call_target="tpu_custom_call" | custom-call | flops 10000000 | bytes 16384000 | tf_op jit(solution)/shard_map/col_reduce/pallas_call | solution.py:267
  416.5 36.6 %fusion.1 = bf16[7168,1000]{0,1:T(8,128)(2,1)} fusion(bf16[4,512,7168]{2,1,0:T(8,128)(2,1)} %param.14, bf16[1,512,1000]{2,1,0:T(8,128)(2,1)} %slice_bitcast_fusion, bf16[1,512,1000]{2,1,0:T(8,128)(2,1)S(1)} %copy-done.9, bf16[1,512,1000]{2,1,0:T(8,128)(2,1)S(1)} %copy-done.8, bf16[1,512,1000]{2,1,0:T(8,128)(2,1)S(1)} %bitcast.155), kind=kOutput, calls=%fused_computation.3 | convolution fusion | flops 29373440000 | bytes 47792128 | tf_op jit(solution)/shard_map/dot_general | solution.py:300
  453.2 6.0 copy.47.tail
  459.2 3.3 pad_maximum_fusion
  462.4 6.3 copy.48
  470.5 39.5 %bitcast_convert_fusion = bf16[1000,14336]{1,0:T(8,128)(2,1)} fusion(bf16[4,256,1000]{1,2,0:T(8,128)(2,1)S(1)} %pad_maximum_fusion.4, bf16[14336,4,256]{2,1,0:T(4,128)(2,1)} %param.19), kind=kOutput, calls=%fused_computation | convolution fusion | flops 29374464000 | bytes 60080128 | tf_op jit(solution)/shard_map/dot_general | solution.py:365
  510.0 38.4 %copy.46 = bf16[1000,14336]{0,1:T(8,128)(2,1)} copy(bf16[1000,14336]{1,0:T(8,128)(2,1)} %bitcast_convert_fusion) | data formatting | bytes 57344000 | tf_op jit(solution)/shard_map/convert_element_type | solution.py:365
  548.4 345.6 %col_scatter.1 = bf16[1792,1000]{1,0:T(8,128)(2,1)S(1)} custom-call(bf16[14336,1000]{1,0:T(8,128)(2,1)} %bitcast.157, bf16[1792,1000]{1,0:T(8,128)(2,1)} %copy.47.tail), custom_call_target="tpu_custom_call" | custom-call | flops 1000000000 | bytes 229376000 | tf_op jit(solution)/shard_map/col_scatter/pallas_call | solution.py:129
  895.9 6.0 copy.49
  901.8 5.8 subtract_convert_fusion
  (76 shorter events, 53.0 us)
Async XLA Ops:
  7.2 85.4 %all-reduce.14.cloned.1.call-start = ((), (), s32[]{:S(2)}) async-start(), calls=%async_computation.5 | async-start | bytes 2048000 | tf_op jit(solution)/shard_map/psum | solution.py:296
  52.1 158.0 %all-reduce.12.cloned.1.call-start = ((), (), s32[]{:S(2)}) async-start(), calls=%async_computation.4 | async-start | bytes 2048000 | tf_op jit(solution)/shard_map/psum | solution.py:296
  99.1 64.9 %copy-start.15 = (f32[1000,256]{1,0:T(8,128)S(1)}, f32[1000,256]{1,0:T(8,128)}, u32[]{:S(2)}) copy-start(f32[1000,256]{1,0:T(8,128)} %fusion.59) | copy-start | bytes 3072004
  164.0 2.3 copy-start.13
  168.6 165.6 %all-reduce.10.cloned.1.call-start = ((), (), s32[]{:S(2)}) async-start(), calls=%async_computation.3 | async-start | bytes 2048000 | tf_op jit(solution)/shard_map/psum | solution.py:296
  210.1 1.6 copy-start.3
  223.1 64.9 %copy-start.14 = (f32[1000,256]{1,0:T(8,128)S(1)}, f32[1000,256]{1,0:T(8,128)}, u32[]{:S(2)}) copy-start(f32[1000,256]{1,0:T(8,128)} %convolution_add_fusion.3) | copy-start | bytes 3072004
  288.0 2.5 copy-start.1
  288.0 2.5 copy-start.12
  292.9 175.8 %all-reduce.8.cloned.1.call-start = ((), (), s32[]{:S(2)}) async-start(), calls=%async_computation.2 | async-start | bytes 1024000 | tf_op jit(solution)/shard_map/psum | solution.py:296
  293.1 2.0 copy-start.2
  295.1 40.7 %copy-start.5 = (bf16[256,1000]{0,1:T(8,128)(2,1)S(1)}, bf16[256,1000]{0,1:T(8,128)(2,1)}, u32[]{:S(2)}) copy-start(bf16[256,1000]{0,1:T(8,128)(2,1)} %get-tuple-element.14) | copy-start | bytes 1536004
  340.5 2.6 copy-start.16
  343.1 4.1 copy-start.7
  412.3 1.6 copy-start.11
  413.9 2.6 copy-start.8
  413.9 2.6 copy-start.9
  416.4 485.4 %reduce-scatter.2.cloned.1.call-start = ((), (), s32[]{:S(2)}) async-start(), calls=%async_computation.1 | async-start | bytes 17920000 | tf_op jit(solution)/shard_map/reduce_scatter | solution.py:354
  462.4 6.3 copy-start.4
  462.4 6.3 copy-start.6
  470.5 39.5 %copy-start.10 = (bf16[4,256,1000]{1,2,0:T(8,128)(2,1)}, bf16[4,256,1000]{1,2,0:T(8,128)(2,1)S(1)}, u32[]{:S(2)}) copy-start(bf16[4,256,1000]{1,2,0:T(8,128)(2,1)S(1)} %pad_maximum_fusion.4) | copy-start | bytes 6144004
  894.1 1.8 copy-start
Sparse Core Ops, SparseCore 0:
  52.2 40.3 all-reduce.13
  168.8 41.2 all-reduce.11
  293.0 41.1 all-reduce.9
  416.6 38.2 all-reduce.7
  457.5 115.0 reduce-scatter.1
